TPU v7x, 256 devices: a whole 4x4x8 slice. The times are simulated.
256 devices in a mesh: seq: 64 (over y, z, core), head: 4 (over x).
Axes of the slice: x: 4, y: 4, z: 8, core: 2. Of those that a mesh axis runs over, the one named last changes fastest.
Arguments:
- queries: bfloat16 [12288, 4096], P('seq', 'head'), may hold values from -10 to 10
- key_states: bfloat16 [12288, 1024], P('seq', 'head'), may hold values from -6 to 6
- value_states: bfloat16 [12288, 1024], P('seq', 'head'), may hold values from -6 to 6
- out_weight: bfloat16 [4096, 4096], P('head'), may hold values from -0.09375 to 0.09375
Outputs:
- mixed: bfloat16 [12288, 4096], P('seq', 'head')
All inputs are finite; a program needn't handle non-finite values.
Results may differ from a plain program's by a relative error of at most 0.02.
Values may be sent and summed in bfloat16 or wider, within the bound.
A program may use at most 128 MiB of HBM per device.

v0:
```python
import jax
import jax.numpy as jnp
from jax import lax
from jax.sharding import PartitionSpec as P

HEADS = 32
KV_HEADS = 8
HEAD_DIM = 128


masked_score = -1e30


def update(state, query_set, query_pos, key_block, value_block, key_pos, keep):
    numerator, running_max, running_sum = state
    columns = key_block.shape[0]
    key_heads = key_block.reshape(columns, -1, HEAD_DIM)
    value_heads = value_block.reshape(columns, -1, HEAD_DIM)
    scores = jnp.einsum(
        "grd,kgd->grk", query_set, key_heads, preferred_element_type=jnp.float32
    ) * HEAD_DIM ** (-0.5)
    allowed = (keep[None, :] & (key_pos[None, :] <= query_pos[:, None]))[None]
    scores = jnp.where(allowed, scores, masked_score)
    highest = jnp.maximum(running_max, jnp.max(scores, axis=2))
    weights = jnp.where(allowed, jnp.exp(scores - highest[:, :, None]), 0.0)
    factor = jnp.exp(running_max - highest)
    running_sum = running_sum * factor + jnp.sum(weights, axis=2)
    numerator = numerator * factor[:, :, None] + jnp.einsum(
        "grk,kgd->grd",
        weights.astype(jnp.bfloat16),
        value_heads,
        preferred_element_type=jnp.float32,
    )
    return (numerator, highest, running_sum)


def process(state, task, key_spans, value_spans, span_ids):
    query_set, query_pos, lowest, highest_span = task
    count, rows, width_cols = key_spans.shape
    grouping = 4
    key_groups = key_spans.reshape(count // grouping, grouping * rows, width_cols)
    value_groups = value_spans.reshape(count // grouping, grouping * rows, width_cols)
    id_groups = span_ids.reshape(count // grouping, grouping)
    offsets = jnp.arange(rows, dtype=jnp.int32)

    def visit(carry, item):
        key_block, value_block, block_ids = item
        wanted = (block_ids > lowest) & (block_ids <= highest_span)
        keep = jnp.repeat(wanted, rows)
        key_pos = (block_ids[:, None] * rows + offsets[None, :]).reshape(-1)
        carry = lax.cond(
            jnp.any(wanted),
            lambda inner: update(
                inner, query_set, query_pos, key_block, value_block, key_pos, keep
            ),
            lambda inner: inner,
            carry,
        )
        return (carry, None)

    state, _ = lax.scan(visit, state, (key_groups, value_groups, id_groups))
    return state


def local(queries, key_states, value_states, out_weight):
    tokens = queries.shape[0]
    local_heads = key_states.shape[1] // HEAD_DIM
    grouping = HEADS // KV_HEADS
    device = lax.axis_index("seq")
    offsets = jnp.arange(tokens, dtype=jnp.int32)
    empty_state = (
        jnp.zeros((local_heads, grouping * tokens, HEAD_DIM), jnp.float32),
        jnp.full((local_heads, grouping * tokens), masked_score, jnp.float32),
        jnp.zeros((local_heads, grouping * tokens), jnp.float32),
    )
    tasks = [
        (
            queries.reshape(tokens, local_heads, grouping, HEAD_DIM)
            .transpose(1, 2, 0, 3)
            .reshape(local_heads, grouping * tokens, HEAD_DIM),
            jnp.tile(device * tokens + offsets, grouping),
            jnp.int32(-1),
            device,
        )
    ]
    states = tuple((empty_state for task in tasks))
    width_cols = key_states.shape[1]
    piece = (
        lax.all_gather(key_states, "seq", axis=0, tiled=True),
        lax.all_gather(value_states, "seq", axis=0, tiled=True),
    )
    count = piece[0].shape[0] // tokens
    span_ids = jnp.arange(count, dtype=jnp.int32)
    key_spans = piece[0].reshape(count, tokens, width_cols)
    value_spans = piece[1].reshape(count, tokens, width_cols)
    states = tuple(
        (
            process(state, task, key_spans, value_spans, span_ids)
            for state, task in zip(states, tasks)
        )
    )
    own_state = states[0]
    attended = own_state[0] / own_state[2][:, :, None]
    attended = attended.reshape(local_heads, grouping, tokens, HEAD_DIM).transpose(2, 0, 1, 3)
    attended = attended.reshape(tokens, local_heads * grouping * HEAD_DIM).astype(jnp.bfloat16)
    projected = jnp.dot(attended, out_weight, preferred_element_type=jnp.float32)
    return lax.psum_scatter(projected.astype(jnp.bfloat16), "head", scatter_dimension=1, tiled=True)


def solution(mesh):
    return jax.shard_map(
        local,
        mesh=mesh,
        in_specs=(P("seq", "head"), P("seq", "head"), P("seq", "head"), P("head", None)),
        out_specs=P("seq", "head"),
        check_vma=False,
    )
```

profile of v0, /device:TPU:1, one launch (start us, length us, event | category | flops | bytes accessed | tf_op | source)
XLA Modules:
  0.0 350.1 jit_solution(4088278459122916354)
XLA Ops:
  6.5 0.7 all-gather.3.cloned.1.call-update
  7.3 0.7 all-gather.5.cloned.1.call-update
  8.1 1.3 reshape.121
  9.4 86.1 %all-gather.3.cloned.1.call-done = bf16[12288,256]{1,0:T(8,128)(2,1)} async-done(((bf16[192,256]{1,0:T(8,128)(2,1)}), bf16[12288,256]{1,0:T(8,128)(2,1)}) %all-gather.3.cloned.1.call-update) | async-done | bytes 6291472 | tf_op jit(solution)/shard_map/all_gather | solution.py:89
  95.5 8.6 %copy.16 = bf16[16,768,256]{1,2,0:T(8,128)(2,1)} copy(bf16[16,768,256]{2,1,0:T(8,128)(2,1)} %bitcast.35) | data formatting | bytes 12582912
  104.1 71.9 %all-gather.5.cloned.1.call-done = bf16[12288,256]{1,0:T(8,128)(2,1)} async-done(((bf16[192,256]{1,0:T(8,128)(2,1)}), bf16[12288,256]{1,0:T(8,128)(2,1)}) %all-gather.5.cloned.1.call-update) | async-done | bytes 6291472 | tf_op jit(solution)/shard_map/all_gather | solution.py:90
  176.0 8.6 %copy.17 = bf16[16,768,256]{1,2,0:T(8,128)(2,1)} copy(bf16[16,768,256]{2,1,0:T(8,128)(2,1)} %bitcast.36) | data formatting | bytes 12582912
  184.7 26.2 %while.15 = (s32[]{:T(128)}, f32[2,768,128]{2,1,0:T(8,128)S(1)}, f32[2,768]{1,0:T(2,128)S(1)}, f32[2,768]{1,0:T(2,128)S(1)}, s32[16,4]{1,0:T(8,128)S(1)}, /*inde...) while((s32[]{:T(128)}, f32[2,768,128]{2,1,0:T(8,128)S(1)}, ...), condition=%wide.region_6.7_spmd.clone, body=%wide.region_0.6_spmd.clone.sunk | while | flops 620891904 | bytes 20969064 | solution.py:61
  184.7 0.6 fusion.23
  185.9 6.9 %conditional.3 = ((f32[2,768,128]{2,1,0:T(8,128)S(1)}, f32[2,768]{1,0:T(2,128)S(1)}, f32[2,768]{1,0:T(2,128)S(1)})) conditional(s32[]{:T(128)} %convert_element_type.36, (f32[2,768,128]{2,1,0:T(8,128)S(1)}, f32[2,768]{1,0:T(2,128)S(1)}, f32[2,768]{1,0:T(2,128)S(1)}) %tuple.45, (pred[1,4]{1,0:T(4,128)(4,1)S(1)}, s32[1,4]{1,0:T(1,128)S(1)}, ...), branch_computations={%region_2.2_spmd, %region_3.5_spmd} | conditional | flops 620891904 | bytes 20968024 | solution.py:51
  186.8 1.2 constant_dynamic-slice_fusion
  188.0 1.2 fusion.4
  189.2 1.2 fusion.5
  190.5 2.3 fusion.10
  195.2 0.6 fusion.23
  196.4 0.6 fusion.23
  197.6 0.6 fusion.23
  198.8 0.6 fusion.23
  200.0 0.6 fusion.23
  207.3 0.6 fusion.23
  208.5 0.6 fusion.23
  209.7 0.6 fusion.23
  211.7 6.3 %convolution_convert_fusion = bf16[192,4096]{1,0:T(8,128)(2,1)} fusion(bf16[192,1024]{1,0:T(8,128)(2,1)S(1)} %convert_element_type.26, bf16[1024,4096]{1,0:T(8,128)(2,1)} %param.11), kind=kOutput, calls=%fused_computation.22 | convolution fusion | flops 1611399168 | bytes 10354688 | tf_op jit(solution)/shard_map/dot_general | solution.py:106
  218.1 125.5 %reduce-scatter.2.cloned.1.call-done = bf16[192,1024]{1,0:T(8,128)(2,1)} async-done(((bf16[192,4096]{1,0:T(8,128)(2,1)}), bf16[192,1024]{1,0:T(8,128)(2,1)}) %reduce-scatter.2.cloned.1.call-update) | async-done | bytes 393232 | tf_op jit(solution)/shard_map/reduce_scatter | solution.py:107
  (62 shorter events, 6.5 us)
Async XLA Ops:
  6.5 89.0 %all-gather.3.cloned.1.call-start = ((), (), s32[]{:S(2)}) async-start(), calls=%async_computation.1 | async-start | bytes 6389760 | tf_op jit(solution)/shard_map/all_gather | solution.py:89
  7.3 168.7 %all-gather.5.cloned.1.call-start = ((), (), s32[]{:S(2)}) async-start(), calls=%async_computation.2 | async-start | bytes 6389760 | tf_op jit(solution)/shard_map/all_gather | solution.py:90
  8.0 335.6 %reduce-scatter.2.cloned.1.call-start = ((), (), s32[]{:S(2)}) async-start(), calls=%async_computation.3 | async-start | bytes 1966080 | tf_op jit(solution)/shard_map/reduce_scatter | solution.py:107
Sparse Core Ops, SparseCore 0:
  10.1 85.3 all-gather.2
  98.3 77.6 all-gather.4
  218.2 125.3 reduce-scatter.1
where the time goes:
time: 351 us; the launch traced here: 350 us
  waiting for transfers between devices  285 us (81%)
  local copies, waits for them, and re-layouts  20.7 us (6%)
  between operations  13.2 us (4%)
  other arithmetic  11.9 us (3%)
  matrix products  9.85 us (3%)
  loops' own time  9.48 us (3%)
    reduce_scatter x1, waiting for transfers between devices, local(): lax.psum_scatter(projected.astype(jnp.bfloat16), 'head', scatter_dimensio...  125 us
    all_gather x1, waiting for transfers between devices, local(): lax.all_gather(key_states, 'seq', axis=0, tiled=True)  86.1 us
    all_gather x1, waiting for transfers between devices, local(): lax.all_gather(value_states, 'seq', axis=0, tiled=True)  71.9 us
    unnamed x2, local copies, waits for them, and re-layouts  17.2 us
    reduce_or x16, other arithmetic, visit(): jnp.any(wanted)  9.85 us
    another operation x1, loops' own time, process(): state, _ = lax.scan(visit, state, (key_groups, value_groups, id_groups))  9.23 us
  transfers between devices with their start and end apart: 3, of which 3 were waited for; matrix products, arithmetic and copies ran while one was open for 3% of the time, Pallas kernels for 0%

commit v1 on v0

v1 whole, which is shorter than its diff:
```python
import jax
import jax.numpy as jnp
from jax import lax
from jax.experimental import pallas as pl
from jax.experimental.pallas import tpu as pltpu
from jax.sharding import PartitionSpec as P

MESH = pl.DeviceIdType.MESH
HEAD_DIM = 128
SCALE = HEAD_DIM ** -0.5 * 1.4426950408889634
NEG = -1e30
T = 192
U = 2 * T
Z = 8
ROWS = 2 * U
TILE = 256


def kernel(
    q_ref, k_ref, v_ref, w_ref, out_ref,
    kv, qraw, qs, acc, top, att, attin, wv, po, pp, pm, ro, fp, fm,
    r_sem, s_sem, sr_sem, ss_sem, ys_sem, own_sem, part_r, part_s,
    q_own, q_r, q_s, w_sem, att_r, att_s, att_own, x_r, x_s,
):
    seq, x = lax.axis_index("seq"), lax.axis_index("head")
    y, z, c = seq // 16, (seq // 2) % Z, seq % 2
    late_home = y // 2
    h = late_home
    outer = jnp.where((y == 0) | (y == 3), 1, 0)
    inner = 1 - outer
    z_up, z_down = (z + 1) % Z, (z + Z - 1) % Z
    y_near = y + 1 - 2 * (y % 2)
    y_pair = 3 - y
    xp, xm, xo = (x + 1) % 4, (x + 3) % 4, (x + 2) % 4

    def dev(yy, zz, cc, xx=None):
        return ((yy * Z + zz) * 2 + cc, x if xx is None else xx)

    up, down = dev(y, z_up, c), dev(y, z_down, c)
    near, sibling = dev(y_near, z, c), dev(y, z, 1 - c)
    pair, pair_cross = dev(y_pair, z, c), dev(y_pair, z, 1 - c)
    x_up, x_down = dev(y, z, c, xp), dev(y, z, c, xm)

    barrier = pltpu.get_barrier_semaphore()
    for other in (up, down, near, sibling, pair, pair_cross, x_up, x_down):
        pl.semaphore_signal(barrier, inc=1, device_id=other, device_id_type=MESH)

    mine = pl.ds(pl.multiple_of(c * T, T), T)

    def block(slot, zz):
        return kv.at[slot, zz, :, mine, :]

    def half(slot, zz, which):
        return kv.at[slot, zz, which, mine, :]

    def remote(src, dst, s, r, to):
        return pltpu.make_async_remote_copy(
            src_ref=src, dst_ref=dst, send_sem=s, recv_sem=r, device_id=to, device_id_type=MESH
        )

    own_slot = 2 * late_home
    other_slot = 2 - own_slot
    own_copies = [
        pltpu.make_async_copy(
            ref.at[:, pl.ds(pl.multiple_of(h * HEAD_DIM, HEAD_DIM), HEAD_DIM)],
            half(own_slot, z, i),
            own_sem.at[i],
        )
        for i, ref in enumerate((k_ref, v_ref))
    ]
    for copy in own_copies:
        copy.start()

    def q_cols(hh, cc):
        return q_ref.at[:, pl.ds(pl.multiple_of(hh * 512 + cc * 256, 256), 256)]

    my_q = pltpu.make_async_copy(q_cols(h, c), qraw.at[late_home, mine, :], q_own)
    my_q.start()
    pl.semaphore_wait(barrier, 8)

    pair_copies = [
        remote(
            ref.at[:, pl.ds(pl.multiple_of((1 - h) * HEAD_DIM, HEAD_DIM), HEAD_DIM)],
            half(own_slot, z, i),
            part_s.at[i],
            part_r.at[i],
            pair,
        )
        for i, ref in enumerate((k_ref, v_ref))
    ]
    for copy in pair_copies:
        copy.start()
    q_copies = [
        remote(q_cols(h, 1 - c), qraw.at[late_home, mine, :], q_s.at[0], q_r.at[0], sibling),
        remote(q_cols(1 - h, c), qraw.at[late_home, mine, :], q_s.at[1], q_r.at[1], pair),
        remote(q_cols(1 - h, 1 - c), qraw.at[late_home, mine, :], q_s.at[2], q_r.at[2], pair_cross),
    ]
    for copy in q_copies:
        copy.start()
    w_copies = [
        pltpu.make_async_copy(
            w_ref.at[:, pl.ds(pl.multiple_of(col * 1024, 1024), 1024)], wv.at[j], w_sem.at[j]
        )
        for j, col in enumerate((xo, xp, xm, x))
    ]
    for copy in w_copies:
        copy.start()

    def hop(slot, zz, msg, to):
        return remote(block(slot, zz), block(slot, zz), s_sem.at[slot, msg], r_sem.at[slot, msg], to)

    def hop_half(slot, zz, which, msg, to):
        return remote(
            half(slot, zz, which), half(slot, zz, which), s_sem.at[slot, msg], r_sem.at[slot, msg], to
        )

    def to_sibling(slot, zz, msg):
        return remote(block(slot, zz), block(slot, zz), ss_sem.at[slot, msg], sr_sem.at[slot, msg], sibling)

    def to_sibling_half(slot, zz, which, msg):
        return remote(
            half(slot, zz, which), half(slot, zz, which), ss_sem.at[slot, msg], sr_sem.at[slot, msg], sibling
        )

    def to_near(zz, msg):
        return remote(block(0, zz), block(1, zz), ys_sem.at[msg], r_sem.at[1, msg], near)

    def to_near_half(zz, which, msg):
        return remote(half(0, zz, which), half(1, zz, which), ys_sem.at[msg], r_sem.at[1, msg], near)

    def late_to_near():
        return remote(block(2, z), block(3, z), ys_sem.at[9], r_sem.at[3, 0], near)

    def from_sibling(slot, zz, msg):
        theirs = pl.ds(pl.multiple_of((1 - c) * T, T), T)
        ref = kv.at[slot, zz, :, theirs, :]
        return remote(ref, ref, ss_sem.at[slot, msg], sr_sem.at[slot, msg], sibling)

    def from_sibling_half(slot, zz, which, msg):
        theirs = pl.ds(pl.multiple_of((1 - c) * T, T), T)
        ref = kv.at[slot, zz, which, theirs, :]
        return remote(ref, ref, ss_sem.at[slot, msg], sr_sem.at[slot, msg], sibling)

    def below(k):
        return (z + Z - k) % Z

    def above(k):
        return (z + k) % Z

    def start_own(slot):
        hop(slot, z, 1, up).start()
        hop(slot, z, 5, down).start()
        to_sibling(slot, z, 0).start()

    for copy in own_copies:
        copy.wait()
    start_own(own_slot)

    @pl.when(late_home == 0)
    def _():
        to_near(z, 0).start()

    @pl.when((late_home == 1) & (inner == 1))
    def _():
        late_to_near().start()

    for i in range(2):
        remote(half(other_slot, z, i), half(other_slot, z, i), part_s.at[i], part_r.at[i], pair).wait_recv()
    start_own(other_slot)

    @pl.when(late_home == 1)
    def _():
        to_near(z, 0).start()

    @pl.when((late_home == 0) & (inner == 1))
    def _():
        late_to_near().start()

    acc[...] = jnp.zeros_like(acc)
    top[...] = jnp.full_like(top, NEG)

    def prepare(group):
        for head in range(2):
            value = qraw[group, :, head * 128 : (head + 1) * 128].astype(jnp.float32) * SCALE
            high = value.astype(jnp.bfloat16)
            low = (value - high.astype(jnp.float32)).astype(jnp.bfloat16)
            qs[group, head * U : (head + 1) * U, 0:128] = high
            qs[group, head * U : (head + 1) * U, 128:256] = low

    my_q.wait()
    their = pl.ds(pl.multiple_of((1 - c) * T, T), T)
    remote(qraw.at[late_home, their, :], qraw.at[late_home, their, :], q_s.at[0], q_r.at[0], sibling).wait_recv()
    remote(qraw.at[1 - late_home, mine, :], qraw.at[1 - late_home, mine, :], q_s.at[1], q_r.at[1], pair).wait_recv()
    remote(
        qraw.at[1 - late_home, their, :], qraw.at[1 - late_home, their, :], q_s.at[2], q_r.at[2], pair_cross
    ).wait_recv()
    prepare(0)
    prepare(1)

    @pl.when(outer == 1)
    def _():
        hop(3, z, 0, near).wait_recv()
        start_own(3)

    hop(1, z, 0, near).wait_recv()
    to_sibling(1, z, 0).start()

    ones = jnp.ones((U, HEAD_DIM), jnp.bfloat16)

    def update(group, tile, scores, values):
        rows = pl.ds(tile * TILE, TILE)
        old = top[group, rows, :]
        new = jnp.maximum(old, jnp.max(scores, axis=1, keepdims=True))
        top[group, rows, :] = new
        factor = jnp.exp2(old - new)
        weights = jnp.exp2(scores - new[:, 0:1]).astype(jnp.bfloat16)
        term = jnp.dot(weights, values, preferred_element_type=jnp.float32)
        acc[group, rows, :] = acc[group, rows, :] * jnp.concatenate([factor, factor], axis=1) + term

    def dot_keys(group, tile, keys):
        return lax.dot_general(
            qs[group, pl.ds(tile * TILE, TILE), :],
            keys,
            (((1,), (1,)), ((), ())),
            preferred_element_type=jnp.float32,
        )

    def item_of(i):
        third = jnp.where(i == 3, 1, 0)
        first = jnp.where(i == 0, 1, 0)
        group = 1 - first - third * inner
        slot = i // 2 + 2 * third * outer
        masked = (i == 0) | (i == 4)
        return group, slot, masked

    def attend_two(k, i):
        group, slot, masked = item_of(i)
        a, b = below(k), above(k)
        keys = jnp.concatenate([kv[slot, a, 0], kv[slot, b, 0]], axis=0)
        keys = jnp.concatenate([keys, keys], axis=1)
        values = jnp.concatenate(
            [
                jnp.concatenate([kv[slot, a, 1], ones], axis=1),
                jnp.concatenate([kv[slot, b, 1], ones], axis=1),
            ],
            axis=0,
        )
        bias_a = jnp.where(masked & (z < k), NEG, 0.0).astype(jnp.float32)
        bias_b = jnp.where(masked & (z + k < Z), NEG, 0.0).astype(jnp.float32)
        column = lax.broadcasted_iota(jnp.int32, (1, 2 * U), 1)
        bias = jnp.where(column < U, bias_a, bias_b)
        for tile in range(ROWS // TILE):
            update(group, tile, dot_keys(group, tile, keys) + bias, values)

    def attend_one(zz, i, diagonal, valid):
        group, slot, masked = item_of(i)
        keys = jnp.concatenate([kv[slot, zz, 0], kv[slot, zz, 0]], axis=1)
        values = jnp.concatenate([kv[slot, zz, 1], ones], axis=1)
        column = lax.broadcasted_iota(jnp.int32, (1, U), 1)
        lift = jnp.where(masked & diagonal, 0, U)
        sink = jnp.where(masked & jnp.logical_not(valid), 4 * U, 0)
        for tile in range(ROWS // TILE):
            row = lax.broadcasted_iota(jnp.int32, (TILE, 1), 0) + tile * TILE
            row = jnp.where(row >= U, row - U, row) + lift - sink
            scores = jnp.where(column <= row, dot_keys(group, tile, keys), NEG)
            update(group, tile, scores, values)

    def attend_two_range(k, low, high):
        def body(i, carry):
            attend_two(k, i)
            return carry

        lax.fori_loop(low, high, body, 0)

    def attend_one_range(zz, low, high, diagonal, valid):
        def body(i, carry):
            attend_one(zz, i, diagonal, valid)
            return carry

        lax.fori_loop(low, high, body, 0)

    def wait_sibling(slot, k):
        from_sibling(slot, below(k), k).wait_recv()
        from_sibling(slot, above(k), k + 4).wait_recv()

    from_sibling(0, z, 0).wait_recv()
    from_sibling(1, z, 0).wait_recv()
    from_sibling(2, z, 0).wait_recv()

    @pl.when(outer == 1)
    def _():
        from_sibling(3, z, 0).wait_recv()

    attend_one_range(z, 0, 5, True, True)

    def pass_on(slot, k):
        a, b = below(k), above(k)
        hop(slot, a, k, down).wait_recv()

        @pl.when(k < 3)
        def _():
            hop(slot, a, k + 1, up).start()

        @pl.when(k == 3)
        def _():
            hop_half(slot, a, 0, 4, up).start()

        to_sibling(slot, a, k).start()
        hop(slot, b, k + 4, up).wait_recv()

        @pl.when(k < 3)
        def _():
            hop(slot, b, k + 5, down).start()

        @pl.when(k == 3)
        def _():
            hop_half(slot, b, 1, 8, down).start()

        to_sibling(slot, b, k + 4).start()

    def step(k, carry):
        pass_on(0, k)
        to_near(below(k), k).start()
        to_near(above(k), k + 4).start()

        @pl.when(k > 1)
        def _():
            wait_sibling(2, k - 1)
            attend_two_range(k - 1, 4, 5)

        @pl.when(outer == 1)
        def _():
            pass_on(3, k)

        wait_sibling(0, k)
        attend_two_range(k, 0, 2)
        pass_on(2, k)
        for msg, zz in ((k, below(k)), (k + 4, above(k))):
            hop(1, zz, msg, near).wait_recv()
            to_sibling(1, zz, msg).start()
        wait_sibling(1, k)

        @pl.when(outer == 1)
        def _():
            wait_sibling(3, k)

        attend_two_range(k, 2, 4)
        return carry

    lax.fori_loop(1, 4, step, 0)

    far = above(4)

    def pass_far(slot, near_too):
        for which, msg, source in ((0, 4, down), (1, 8, up)):
            hop_half(slot, far, which, msg, source).wait_recv()
            to_sibling_half(slot, far, which, msg).start()
            if near_too:
                to_near_half(far, which, msg).start()

    def wait_far(slot):
        from_sibling_half(slot, far, 0, 4).wait_recv()
        from_sibling_half(slot, far, 1, 8).wait_recv()

    pass_far(0, True)
    wait_sibling(2, 3)
    attend_two_range(3, 4, 5)

    @pl.when(outer == 1)
    def _():
        pass_far(3, False)

    pass_far(2, False)
    pass_far(1, False)
    for slot in (0, 1, 2):
        wait_far(slot)

    @pl.when(outer == 1)
    def _():
        wait_far(3)

    attend_one_range(far, 0, 5, False, z >= 4)

    my_cols = pl.ds(pl.multiple_of(h * 512 + c * 256, 256), 256)

    def finish(group):
        for head in range(2):
            rows = slice(head * U, (head + 1) * U)
            value = acc[group, rows, 0:128] / acc[group, rows, 128:256]
            att[group, :, head * 128 : (head + 1) * 128] = value.astype(jnp.bfloat16)

    def att_to(group, part, to, s, r):
        rows = pl.ds(pl.multiple_of(part * T, T), T)
        return remote(att.at[group, rows, :], attin.at[:, my_cols], s, r, to)

    finish(0)
    finish(1)
    away = 1 - late_home
    sends = [
        att_to(away, c, pair, att_s.at[0], att_r.at[0]),
        att_to(away, 1 - c, pair_cross, att_s.at[1], att_r.at[1]),
        att_to(late_home, 1 - c, sibling, att_s.at[2], att_r.at[2]),
    ]
    for copy in sends:
        copy.start()
    keep = pltpu.make_async_copy(att.at[late_home, mine, :], attin.at[:, my_cols], att_own)
    keep.start()
    keep.wait()
    for index, (hh, cc, source) in enumerate(((1 - h, c, pair), (1 - h, 1 - c, pair_cross), (h, 1 - c, sibling))):
        cols = pl.ds(pl.multiple_of(hh * 512 + cc * 256, 256), 256)
        remote(attin.at[:, cols], attin.at[:, cols], att_s.at[index], att_r.at[index], source).wait_recv()
    for copy in w_copies:
        copy.wait()

    def project(j, store):
        for part in range(4):
            cols = slice(part * 256, (part + 1) * 256)
            store(cols, jnp.dot(attin[...], wv[j, :, cols], preferred_element_type=jnp.float32))

    def into(ref):
        def store(cols, value):
            ref[:, cols] = value.astype(jnp.bfloat16)

        return store

    H = T // 2
    first, second = pl.ds(0, H), pl.ds(H, H)
    project(0, into(po.at[0]))
    far_up = remote(po.at[0, first, :], ro.at[0], x_s.at[0], x_r.at[0], x_up)
    far_down = remote(po.at[0, second, :], ro.at[1], x_s.at[1], x_r.at[1], x_down)
    far_up.start()
    far_down.start()
    project(1, into(pp))
    up_second = remote(pp.at[second, :], fp.at[second, :], x_s.at[2], x_r.at[2], x_up)
    up_second.start()
    project(2, into(pm))
    down_first = remote(pm.at[first, :], fm.at[first, :], x_s.at[3], x_r.at[3], x_down)
    down_first.start()
    far_up.wait_recv()
    pp[0:H, :] = (pp[0:H, :].astype(jnp.float32) + ro[0].astype(jnp.float32)).astype(jnp.bfloat16)
    up_first = remote(pp.at[first, :], fp.at[first, :], x_s.at[4], x_r.at[4], x_up)
    up_first.start()
    far_down.wait_recv()
    pm[H:T, :] = (pm[H:T, :].astype(jnp.float32) + ro[1].astype(jnp.float32)).astype(jnp.bfloat16)
    down_second = remote(pm.at[second, :], fm.at[second, :], x_s.at[5], x_r.at[5], x_down)
    down_second.start()
    project(3, into(po.at[1]))
    for copy in (up_second, down_first, up_first, down_second):
        copy.wait_recv()
    total = po[1].astype(jnp.float32) + fp[...].astype(jnp.float32) + fm[...].astype(jnp.float32)
    out_ref[...] = total.astype(jnp.bfloat16)

    for copy in (far_up, far_down, up_second, down_first, up_first, down_second, *sends, *pair_copies, *q_copies):
        copy.wait_send()

    def sent(slot):
        def whole(k, carry):
            hop(slot, z, k, up).wait_send()
            hop(slot, z, k + 4, down).wait_send()
            to_sibling(slot, z, k).wait_send()
            to_sibling(slot, z, k + 4).wait_send()
            return carry

        lax.fori_loop(1, 4, whole, 0)
        to_sibling(slot, z, 0).wait_send()
        hop_half(slot, z, 0, 4, up).wait_send()
        hop_half(slot, z, 1, 8, down).wait_send()
        to_sibling_half(slot, z, 0, 4).wait_send()
        to_sibling_half(slot, z, 1, 8).wait_send()

    sent(0)
    sent(2)

    @pl.when(outer == 1)
    def _():
        sent(3)

    @pl.when(inner == 1)
    def _():
        late_to_near().wait_send()

    def near_sent(k, carry):
        to_near(z, k).wait_send()
        to_near(z, k + 4).wait_send()
        to_sibling(1, z, k).wait_send()
        to_sibling(1, z, k + 4).wait_send()
        return carry

    lax.fori_loop(1, 4, near_sent, 0)
    to_near(z, 0).wait_send()
    to_sibling(1, z, 0).wait_send()
    to_near_half(z, 0, 4).wait_send()
    to_near_half(z, 1, 8).wait_send()
    to_sibling_half(1, z, 0, 4).wait_send()
    to_sibling_half(1, z, 1, 8).wait_send()


def local(queries, key_states, value_states, out_weight):
    bf16, f32 = jnp.bfloat16, jnp.float32
    any_spec = pl.BlockSpec(memory_space=pl.ANY)
    dma = pltpu.SemaphoreType.DMA
    return pl.pallas_call(
        kernel,
        out_shape=jax.ShapeDtypeStruct((T, 1024), bf16),
        in_specs=[any_spec] * 4,
        out_specs=pl.BlockSpec(memory_space=pltpu.VMEM),
        scratch_shapes=[
            pltpu.VMEM((4, Z, 2, U, HEAD_DIM), bf16),
            pltpu.VMEM((2, U, 256), bf16),
            pltpu.VMEM((2, ROWS, 256), bf16),
            pltpu.VMEM((2, ROWS, 256), f32),
            pltpu.VMEM((2, ROWS, HEAD_DIM), f32),
            pltpu.VMEM((2, U, 256), bf16),
            pltpu.VMEM((T, 1024), bf16),
            pltpu.VMEM((4, 1024, 1024), bf16),
            pltpu.VMEM((2, T, 1024), bf16),
            pltpu.VMEM((T, 1024), bf16),
            pltpu.VMEM((T, 1024), bf16),
            pltpu.VMEM((2, T // 2, 1024), bf16),
            pltpu.VMEM((T, 1024), bf16),
            pltpu.VMEM((T, 1024), bf16),
            dma((4, 9)), dma((4, 9)), dma((4, 9)), dma((4, 9)),
            dma((10,)), dma((2,)), dma((2,)), dma((2,)),
            dma, dma((3,)), dma((3,)), dma((4,)),
            dma((3,)), dma((3,)), dma, dma((6,)), dma((6,)),
        ],
        compiler_params=pltpu.CompilerParams(
            collective_id=0, has_side_effects=True, vmem_limit_bytes=48 << 20
        ),
    )(queries, key_states, value_states, out_weight)


def solution(mesh):
    return jax.shard_map(
        local,
        mesh=mesh,
        in_specs=(P("seq", "head"), P("seq", "head"), P("seq", "head"), P("head", None)),
        out_specs=P("seq", "head"),
        check_vma=False,
    )
```

time: 351 us -> 92.2 us (0.26)
  waiting for transfers between devices: 285 us -> 0 us
  Pallas kernels: 0 us -> 88.5 us
  local copies, waits for them, and re-layouts: 20.7 us -> 3.53 us
  between operations: 13.2 us -> 0.01 us
  other arithmetic: 11.9 us -> 0 us
  matrix products: 9.85 us -> 0 us
  loops' own time: 9.48 us -> 0 us
    all_gather x2 -> x0, waiting for transfers between devices: 158 us -> none  [the longest x1 86.1 us: local(): lax.all_gather(key_states, 'seq', axis=0, tiled=True)]
    reduce_scatter x1 -> x0, waiting for transfers between devices: 125 us -> none  [local(): lax.psum_scatter(projected.astype(jnp.bfloat16), 'head', scatter_dimensio...]
    pallas_call x0 -> x1, Pallas kernels: none -> 88.5 us  [local(): pl.pallas_call(kernel, out_shape=jax.ShapeDtypeStruct((T, 1024), bf16), i...]
    unnamed x2 -> x7, local copies, waits for them, and re-layouts: 17.2 us -> 3.53 us
    reduce_or x16 -> x0, other arithmetic: 9.85 us -> none  [visit(): jnp.any(wanted)]
    dot_general x3 -> x0, matrix products: 9.85 us -> none  [the longest x1 6.35 us: local(): jnp.dot(attended, out_weight, preferred_element_type=jnp.float32)]
    another operation x17 -> x0, loops' own time: 9.48 us -> none  [the longest x1 9.23 us: process(): state, _ = lax.scan(visit, state, (key_groups, value_groups, id_groups))]
  transfers between devices with their start and end apart: 3 -> 0, of which waited for: 3 -> 0; matrix products, arithmetic and copies ran while one was open for 3% -> 0% of each run, Pallas kernels for 0% -> 0%
where the time goes in v1:
time: 92.2 us; the launch traced here: 92 us
  Pallas kernels  88.5 us (96%)
  local copies, waits for them, and re-layouts  3.53 us (4%)
    pallas_call x1, Pallas kernels, local(): pl.pallas_call(kernel, out_shape=jax.ShapeDtypeStruct((T, 1024), bf16), i...  88.5 us
    unnamed x7, local copies, waits for them, and re-layouts  3.53 us

profile of v1, /device:TPU:1, one launch (start us, length us, event | category | flops | bytes accessed | tf_op | source)
XLA Modules:
  0.0 92.0 jit_solution(3526865554423551192)
XLA Ops:
  0.0 0.0 copy-start
  0.0 1.0 %copy-done = bf16[192,1024]{1,0:T(8,128)(2,1)S(1)} copy-done((bf16[192,1024]{1,0:T(8,128)(2,1)S(1)}, bf16[192,1024]{1,0:T(8,128)(2,1)}, u32[]{:S(2)}) %copy-start) | copy-done | bytes 393240
  1.0 0.0 copy-start.1
  1.0 0.9 copy-done.1
  1.9 0.0 copy-start.2
  1.9 0.9 copy-done.2
  2.8 88.5 %shard_map.46 = bf16[192,1024]{1,0:T(8,128)(2,1)S(1)} custom-call(bf16[192,1024]{1,0:T(8,128)(2,1)S(1)} %copy-done, bf16[192,256]{1,0:T(8,128)(2,1)S(1)} %copy-done.1, bf16[192,256]{1,0:T(8,128)(2,1)S(1)} %copy-done.2, bf16[1024,4096]{1,0:T(8,128)(2,1)} %w_ref.1), custom_call_target="tpu_custom_call" | custom-call | tf_op jit(solution)/shard_map/pallas_call | solution.py:502
  91.3 0.7 copy.6
Async XLA Ops:
  0.0 1.0 %copy-start = (bf16[192,1024]{1,0:T(8,128)(2,1)S(1)}, bf16[192,1024]{1,0:T(8,128)(2,1)}, u32[]{:S(2)}) copy-start(bf16[192,1024]{1,0:T(8,128)(2,1)} %q_ref.1) | copy-start | bytes 1179652
  1.0 0.9 copy-start.1
  1.9 0.9 copy-start.2

commit v2 on v1

v2 whole, which is shorter than its diff:
```python
import jax
import jax.numpy as jnp
from jax import lax
from jax.experimental import pallas as pl
from jax.experimental.pallas import tpu as pltpu
from jax.sharding import PartitionSpec as P

MESH = pl.DeviceIdType.MESH
HEAD_DIM = 128
SCALE = HEAD_DIM ** -0.5 * 1.4426950408889634
NEG = -1e30
T = 192
U = 2 * T
Z = 8
ROWS = 2 * U
TILE = 256


def kernel(
    q_ref, k_ref, v_ref, w_ref, out_ref,
    kv, qraw, qs, acc, top, att, attin, wv, po, pp, pm, ro, fp, fm,
    r_sem, s_sem, sr_sem, ss_sem, ys_sem, own_sem, part_r, part_s,
    q_own, q_r, q_s, across_r, across_s, w_sem, att_r, att_s, att_own, x_r, x_s,
):
    seq, x = lax.axis_index("seq"), lax.axis_index("head")
    y, z, c = seq // 16, (seq // 2) % Z, seq % 2
    late_home = y // 2
    h = late_home
    outer = jnp.where((y == 0) | (y == 3), 1, 0)
    inner = 1 - outer
    z_up, z_down = (z + 1) % Z, (z + Z - 1) % Z
    y_near = y + 1 - 2 * (y % 2)
    y_pair = 3 - y
    xp, xm, xo = (x + 1) % 4, (x + 3) % 4, (x + 2) % 4

    def dev(yy, zz, cc, xx=None):
        return ((yy * Z + zz) * 2 + cc, x if xx is None else xx)

    up, down = dev(y, z_up, c), dev(y, z_down, c)
    near, sibling = dev(y_near, z, c), dev(y, z, 1 - c)
    pair, pair_cross = dev(y_pair, z, c), dev(y_pair, z, 1 - c)
    across = dev((y + 2) % 4, z, c)
    x_up, x_down = dev(y, z, c, xp), dev(y, z, c, xm)

    barrier = pltpu.get_barrier_semaphore()
    for other in (up, down, near, sibling, pair, pair_cross, across, x_up, x_down):
        pl.semaphore_signal(barrier, inc=1, device_id=other, device_id_type=MESH)

    mine = pl.ds(pl.multiple_of(c * T, T), T)

    def block(slot, zz):
        return kv.at[slot, zz, :, mine, :]

    def half(slot, zz, which):
        return kv.at[slot, zz, which, mine, :]

    def remote(src, dst, s, r, to):
        return pltpu.make_async_remote_copy(
            src_ref=src, dst_ref=dst, send_sem=s, recv_sem=r, device_id=to, device_id_type=MESH
        )

    own_slot = 2 * late_home
    other_slot = 2 - own_slot
    own_copies = [
        pltpu.make_async_copy(
            ref.at[:, pl.ds(pl.multiple_of(h * HEAD_DIM, HEAD_DIM), HEAD_DIM)],
            half(own_slot, z, i),
            own_sem.at[i],
        )
        for i, ref in enumerate((k_ref, v_ref))
    ]
    for copy in own_copies:
        copy.start()

    def q_cols(hh, cc):
        return q_ref.at[:, pl.ds(pl.multiple_of(hh * 512 + cc * 256, 256), 256)]

    my_q = pltpu.make_async_copy(q_cols(h, c), qraw.at[late_home, mine, :], q_own)
    my_q.start()
    pl.semaphore_wait(barrier, 9)

    pair_copies = [
        remote(
            ref.at[:, pl.ds(pl.multiple_of((1 - h) * HEAD_DIM, HEAD_DIM), HEAD_DIM)],
            half(own_slot, z, i),
            part_s.at[i],
            part_r.at[i],
            pair,
        )
        for i, ref in enumerate((k_ref, v_ref))
    ]
    for copy in pair_copies:
        copy.start()
    w_copies = [
        pltpu.make_async_copy(
            w_ref.at[:, pl.ds(pl.multiple_of(col * 1024, 1024), 1024)], wv.at[j], w_sem.at[j]
        )
        for j, col in enumerate((xo, xp, xm, x))
    ]
    def hop(slot, zz, msg, to):
        return remote(block(slot, zz), block(slot, zz), s_sem.at[slot, msg], r_sem.at[slot, msg], to)

    def hop_half(slot, zz, which, msg, to):
        return remote(
            half(slot, zz, which), half(slot, zz, which), s_sem.at[slot, msg], r_sem.at[slot, msg], to
        )

    def to_sibling(slot, zz, msg):
        return remote(block(slot, zz), block(slot, zz), ss_sem.at[slot, msg], sr_sem.at[slot, msg], sibling)

    def to_sibling_half(slot, zz, which, msg):
        return remote(
            half(slot, zz, which), half(slot, zz, which), ss_sem.at[slot, msg], sr_sem.at[slot, msg], sibling
        )

    def to_near(zz, msg):
        return remote(block(0, zz), block(1, zz), ys_sem.at[msg], r_sem.at[1, msg], near)

    def to_near_half(zz, which, msg):
        return remote(half(0, zz, which), half(1, zz, which), ys_sem.at[msg], r_sem.at[1, msg], near)

    def late_to_near():
        return remote(block(2, z), block(3, z), ys_sem.at[9], r_sem.at[3, 0], near)

    def from_sibling(slot, zz, msg):
        theirs = pl.ds(pl.multiple_of((1 - c) * T, T), T)
        ref = kv.at[slot, zz, :, theirs, :]
        return remote(ref, ref, ss_sem.at[slot, msg], sr_sem.at[slot, msg], sibling)

    def from_sibling_half(slot, zz, which, msg):
        theirs = pl.ds(pl.multiple_of((1 - c) * T, T), T)
        ref = kv.at[slot, zz, which, theirs, :]
        return remote(ref, ref, ss_sem.at[slot, msg], sr_sem.at[slot, msg], sibling)

    def below(k):
        return (z + Z - k) % Z

    def above(k):
        return (z + k) % Z

    def start_own(slot):
        hop(slot, z, 1, up).start()
        hop(slot, z, 5, down).start()
        to_sibling(slot, z, 0).start()

    def across_copy(i, ref):
        return remote(
            ref.at[:, pl.ds(pl.multiple_of((1 - h) * HEAD_DIM, HEAD_DIM), HEAD_DIM)],
            half(3, z, i),
            across_s.at[i],
            across_r.at[i],
            across,
        )

    @pl.when(y == 2)
    def _():
        for i, ref in enumerate((k_ref, v_ref)):
            across_copy(i, ref).start()

    for copy in own_copies:
        copy.wait()
    start_own(own_slot)

    @pl.when(late_home == 0)
    def _():
        to_near(z, 0).start()

    @pl.when(y == 2)
    def _():
        late_to_near().start()

    q_copies = [
        remote(q_cols(h, 1 - c), qraw.at[late_home, mine, :], q_s.at[0], q_r.at[0], sibling),
        remote(q_cols(1 - h, c), qraw.at[late_home, mine, :], q_s.at[1], q_r.at[1], pair),
        remote(q_cols(1 - h, 1 - c), qraw.at[late_home, mine, :], q_s.at[2], q_r.at[2], pair_cross),
    ]
    for copy in q_copies:
        copy.start()
    acc[...] = jnp.zeros_like(acc)
    top[...] = jnp.full_like(top, NEG)
    for i in range(2):
        remote(half(other_slot, z, i), half(other_slot, z, i), part_s.at[i], part_r.at[i], pair).wait_recv()
    start_own(other_slot)

    @pl.when(late_home == 1)
    def _():
        to_near(z, 0).start()

    for copy in w_copies:
        copy.start()

    def prepare(group):
        for head in range(2):
            value = qraw[group, :, head * 128 : (head + 1) * 128].astype(jnp.float32) * SCALE
            high = value.astype(jnp.bfloat16)
            low = (value - high.astype(jnp.float32)).astype(jnp.bfloat16)
            qs[group, head * U : (head + 1) * U, 0:128] = high
            qs[group, head * U : (head + 1) * U, 128:256] = low

    def queries_ready():
        my_q.wait()
        their = pl.ds(pl.multiple_of((1 - c) * T, T), T)
        for index, (group, rows, source) in enumerate(
            ((late_home, their, sibling), (1 - late_home, mine, pair), (1 - late_home, their, pair_cross))
        ):
            ref = qraw.at[group, rows, :]
            remote(ref, ref, q_s.at[index], q_r.at[index], source).wait_recv()
        prepare(0)
        prepare(1)

    def update(group, tile, scores, values):
        rows = pl.ds(tile * TILE, TILE)
        old = top[group, rows, :]
        new = jnp.maximum(old, jnp.max(scores, axis=1, keepdims=True))
        top[group, rows, :] = new
        factor = jnp.exp2(old - new)
        weights = jnp.exp2(scores - new[:, 0:1]).astype(jnp.bfloat16)
        term = jnp.dot(weights, values, preferred_element_type=jnp.float32)
        acc[group, rows, :] = acc[group, rows, :] * jnp.concatenate([factor, factor], axis=1) + term

    def dot_keys(group, tile, keys):
        return lax.dot_general(
            qs[group, pl.ds(tile * TILE, TILE), :],
            keys,
            (((1,), (1,)), ((), ())),
            preferred_element_type=jnp.float32,
        )

    def attend(group, pieces, fix=None):
        keys = jnp.concatenate([kv[slot, zz, 0] for slot, zz in pieces], axis=0)
        keys = jnp.concatenate([keys, keys], axis=1)
        values = jnp.concatenate([kv[slot, zz, 1] for slot, zz in pieces], axis=0)
        values = jnp.concatenate([values, jnp.ones_like(values)], axis=1)
        for tile in range(ROWS // TILE):
            scores = dot_keys(group, tile, keys)
            if fix is not None:
                scores = fix(scores, tile)
            update(group, tile, scores, values)

    def with_open(scores, open_cols, tail):
        if open_cols == 0:
            return tail
        return jnp.concatenate([scores[:, :open_cols], tail], axis=1)

    def shut(open_cols, *conditions):
        biases = [jnp.where(condition, NEG, 0.0).astype(jnp.float32) for condition in conditions]

        def fix(scores, tile):
            parts = [
                scores[:, open_cols + i * U : open_cols + (i + 1) * U] + bias for i, bias in enumerate(biases)
            ]
            return with_open(scores, open_cols, jnp.concatenate(parts, axis=1))

        return fix

    def diagonal(open_cols):
        def fix(scores, tile):
            column = lax.broadcasted_iota(jnp.int32, (1, U), 1)
            row = lax.broadcasted_iota(jnp.int32, (TILE, 1), 0) + tile * TILE
            row = jnp.where(row >= U, row - U, row)
            return with_open(scores, open_cols, jnp.where(column <= row, scores[:, open_cols:], NEG))

        return fix

    def wait_sibling(slot, k):
        from_sibling(slot, below(k), k).wait_recv()
        from_sibling(slot, above(k), k + 4).wait_recv()

    def pass_on(slot, k):
        for zz, msg, source, onward, to in ((below(k), k, down, 4, up), (above(k), k + 4, up, 8, down)):
            hop(slot, zz, msg, source).wait_recv()

            @pl.when(k < 3)
            def _(zz=zz, msg=msg, to=to):
                hop(slot, zz, msg + 1, to).start()

            @pl.when(k == 3)
            def _(zz=zz, onward=onward, to=to):
                hop_half(slot, zz, onward // 4 - 1, onward, to).start()

            to_sibling(slot, zz, msg).start()
            if slot == 0:
                to_near(zz, msg).start()

    far = above(4)

    def pass_far(slot):
        for which, msg, source in ((0, 4, down), (1, 8, up)):
            hop_half(slot, far, which, msg, source).wait_recv()
            to_sibling_half(slot, far, which, msg).start()
            if slot == 0:
                to_near_half(far, which, msg).start()

    def wait_far(slot):
        from_sibling_half(slot, far, 0, 4).wait_recv()
        from_sibling_half(slot, far, 1, 8).wait_recv()

    @pl.when(y == 3)
    def _():
        hop(3, z, 0, near).wait_recv()
        start_own(3)

    pass_on(0, 1)

    @pl.when(y == 0)
    def _():
        for i in range(2):
            remote(half(3, z, i), half(3, z, i), across_s.at[i], across_r.at[i], across).wait_recv()
        start_own(3)

    hop(1, z, 0, near).wait_recv()
    to_sibling(1, z, 0).start()
    queries_ready()
    from_sibling(0, z, 0).wait_recv()
    attend(0, [(0, z)], diagonal(0))

    @pl.when(outer == 1)
    def _():
        from_sibling(3, z, 0).wait_recv()
        attend(1, [(0, z), (3, z)])
        from_sibling(1, z, 0).wait_recv()

    @pl.when(inner == 1)
    def _():
        attend(1, [(0, z)])
        from_sibling(1, z, 0).wait_recv()
        attend(0, [(1, z)])

    pass_on(0, 2)
    from_sibling(2, z, 0).wait_recv()
    attend(1, [(1, z), (2, z)], diagonal(U))

    def step(k, carry):
        a, b = below(k), above(k)

        @pl.when(outer == 1)
        def _():
            pass_on(3, k)

        wait_sibling(0, k)
        attend(0, [(0, a), (0, b)], shut(0, z < k, z + k < Z))
        pass_on(2, k)
        for msg, zz in ((k, a), (k + 4, b)):
            hop(1, zz, msg, near).wait_recv()
            to_sibling(1, zz, msg).start()

        @pl.when(outer == 1)
        def _():
            wait_sibling(3, k)
            attend(1, [(0, a), (0, b), (3, a), (3, b)])
            wait_sibling(1, k)

        @pl.when(inner == 1)
        def _():
            attend(1, [(0, a), (0, b)])
            wait_sibling(1, k)
            attend(0, [(1, a), (1, b)])

        @pl.when(k == 1)
        def _():
            pass_on(0, 3)

        @pl.when(k == 2)
        def _():
            pass_far(0)

        @pl.when(k == 3)
        def _():
            pass_far(1)

        wait_sibling(2, k)
        attend(1, [(1, a), (1, b), (2, a), (2, b)], shut(2 * U, z < k, z + k < Z))
        return carry

    lax.fori_loop(1, 4, step, 0)

    wait_far(0)
    attend(0, [(0, far)], shut(0, z < 4))

    @pl.when(outer == 1)
    def _():
        pass_far(3)

    pass_far(2)
    wait_far(1)

    @pl.when(outer == 1)
    def _():
        wait_far(3)
        attend(1, [(0, far), (3, far)])

    @pl.when(inner == 1)
    def _():
        attend(1, [(0, far)])
        attend(0, [(1, far)])

    my_cols = pl.ds(pl.multiple_of(h * 512 + c * 256, 256), 256)
    H = T // 2

    def finish(group, part):
        for core in range(2):
            start = core * T + part * H
            for head in range(2):
                rows = slice(head * U + start, head * U + start + H)
                value = acc[group, rows, 0:128] / acc[group, rows, 128:256]
                att[group, start : start + H, head * 128 : (head + 1) * 128] = value.astype(jnp.bfloat16)

    def att_rows(core, part):
        return pl.ds(pl.multiple_of(core * T + part * H, 32), H)

    def att_to(index, group, core, part, to):
        return remote(
            att.at[group, att_rows(core, part), :],
            attin.at[pl.ds(part * H, H), my_cols],
            att_s.at[index, part],
            att_r.at[index, part],
            to,
        )

    def att_keep(part):
        return pltpu.make_async_copy(
            att.at[late_home, att_rows(c, part), :], attin.at[pl.ds(part * H, H), my_cols], att_own.at[part]
        )

    def send_attended(group, part):
        finish(group, part)

        @pl.when(late_home == group)
        def _():
            att_to(2, group, 1 - c, part, sibling).start()
            att_keep(part).start()

        @pl.when(late_home != group)
        def _():
            att_to(0, group, c, part, pair).start()
            att_to(1, group, 1 - c, part, pair_cross).start()

    def attended_ready(part):
        att_keep(part).wait()
        for index, (hh, cc, source) in enumerate(
            ((1 - h, c, pair), (1 - h, 1 - c, pair_cross), (h, 1 - c, sibling))
        ):
            cols = pl.ds(pl.multiple_of(hh * 512 + cc * 256, 256), 256)
            ref = attin.at[pl.ds(part * H, H), cols]
            remote(ref, ref, att_s.at[index, part], att_r.at[index, part], source).wait_recv()

    for part in range(2):
        send_attended(0, part)
    wait_far(2)
    attend(1, [(1, far), (2, far)], shut(U, z < 4))
    for part in range(2):
        send_attended(1, part)
    for copy in w_copies:
        copy.wait()

    def project(j, part, ref):
        rows = slice(part * H, (part + 1) * H)
        for piece in range(4):
            cols = slice(piece * 256, (piece + 1) * 256)
            value = jnp.dot(attin[rows, :], wv[j, :, cols], preferred_element_type=jnp.float32)
            ref[rows, cols] = value.astype(jnp.bfloat16)

    first, second = pl.ds(0, H), pl.ds(H, H)
    far_up = remote(po.at[0, first, :], ro.at[0], x_s.at[0], x_r.at[0], x_up)
    far_down = remote(po.at[0, second, :], ro.at[1], x_s.at[1], x_r.at[1], x_down)
    up_second = remote(pp.at[second, :], fp.at[second, :], x_s.at[2], x_r.at[2], x_up)
    down_first = remote(pm.at[first, :], fm.at[first, :], x_s.at[3], x_r.at[3], x_down)
    up_first = remote(pp.at[first, :], fp.at[first, :], x_s.at[4], x_r.at[4], x_up)
    down_second = remote(pm.at[second, :], fm.at[second, :], x_s.at[5], x_r.at[5], x_down)
    attended_ready(0)
    project(0, 0, po.at[0])
    far_up.start()
    project(2, 0, pm)
    down_first.start()
    attended_ready(1)
    project(0, 1, po.at[0])
    far_down.start()
    project(1, 1, pp)
    up_second.start()
    project(1, 0, pp)
    far_up.wait_recv()
    pp[0:H, :] = (pp[0:H, :].astype(jnp.float32) + ro[0].astype(jnp.float32)).astype(jnp.bfloat16)
    up_first.start()
    project(2, 1, pm)
    far_down.wait_recv()
    pm[H:T, :] = (pm[H:T, :].astype(jnp.float32) + ro[1].astype(jnp.float32)).astype(jnp.bfloat16)
    down_second.start()
    project(3, 0, po.at[1])
    project(3, 1, po.at[1])

    def total(part):
        rows = slice(part * H, (part + 1) * H)
        value = po[1, rows, :].astype(jnp.float32) + fp[rows, :].astype(jnp.float32)
        out_ref[rows, :] = (value + fm[rows, :].astype(jnp.float32)).astype(jnp.bfloat16)

    down_first.wait_recv()
    up_first.wait_recv()
    total(0)
    up_second.wait_recv()
    down_second.wait_recv()
    total(1)

    for copy in (far_up, far_down, up_second, down_first, up_first, down_second, *pair_copies, *q_copies):
        copy.wait_send()

    for part in range(2):
        att_to(0, 0, c, part, pair).wait_send()
        att_to(1, 0, 1 - c, part, pair_cross).wait_send()
        att_to(2, 0, 1 - c, part, sibling).wait_send()

    def sent(slot):
        def whole(k, carry):
            hop(slot, z, k, up).wait_send()
            hop(slot, z, k + 4, down).wait_send()
            to_sibling(slot, z, k).wait_send()
            to_sibling(slot, z, k + 4).wait_send()
            return carry

        lax.fori_loop(1, 4, whole, 0)
        to_sibling(slot, z, 0).wait_send()
        hop_half(slot, z, 0, 4, up).wait_send()
        hop_half(slot, z, 1, 8, down).wait_send()
        to_sibling_half(slot, z, 0, 4).wait_send()
        to_sibling_half(slot, z, 1, 8).wait_send()

    sent(0)
    sent(2)

    @pl.when(outer == 1)
    def _():
        sent(3)

    @pl.when(y == 2)
    def _():
        late_to_near().wait_send()
        for i, ref in enumerate((k_ref, v_ref)):
            across_copy(i, ref).wait_send()

    def near_sent(k, carry):
        to_near(z, k).wait_send()
        to_near(z, k + 4).wait_send()
        to_sibling(1, z, k).wait_send()
        to_sibling(1, z, k + 4).wait_send()
        return carry

    lax.fori_loop(1, 4, near_sent, 0)
    to_near(z, 0).wait_send()
    to_sibling(1, z, 0).wait_send()
    to_near_half(z, 0, 4).wait_send()
    to_near_half(z, 1, 8).wait_send()
    to_sibling_half(1, z, 0, 4).wait_send()
    to_sibling_half(1, z, 1, 8).wait_send()


def local(queries, key_states, value_states, out_weight):
    bf16, f32 = jnp.bfloat16, jnp.float32
    any_spec = pl.BlockSpec(memory_space=pl.ANY)
    dma = pltpu.SemaphoreType.DMA
    return pl.pallas_call(
        kernel,
        out_shape=jax.ShapeDtypeStruct((T, 1024), bf16),
        in_specs=[any_spec] * 4,
        out_specs=pl.BlockSpec(memory_space=pltpu.VMEM),
        scratch_shapes=[
            pltpu.VMEM((4, Z, 2, U, HEAD_DIM), bf16),
            pltpu.VMEM((2, U, 256), bf16),
            pltpu.VMEM((2, ROWS, 256), bf16),
            pltpu.VMEM((2, ROWS, 256), f32),
            pltpu.VMEM((2, ROWS, HEAD_DIM), f32),
            pltpu.VMEM((2, U, 256), bf16),
            pltpu.VMEM((T, 1024), bf16),
            pltpu.VMEM((4, 1024, 1024), bf16),
            pltpu.VMEM((2, T, 1024), bf16),
            pltpu.VMEM((T, 1024), bf16),
            pltpu.VMEM((T, 1024), bf16),
            pltpu.VMEM((2, T // 2, 1024), bf16),
            pltpu.VMEM((T, 1024), bf16),
            pltpu.VMEM((T, 1024), bf16),
            dma((4, 9)), dma((4, 9)), dma((4, 9)), dma((4, 9)),
            dma((10,)), dma((2,)), dma((2,)), dma((2,)),
            dma, dma((3,)), dma((3,)), dma((2,)), dma((2,)), dma((4,)),
            dma((3, 2)), dma((3, 2)), dma((2,)), dma((6,)), dma((6,)),
        ],
        compiler_params=pltpu.CompilerParams(
            collective_id=0, has_side_effects=True, vmem_limit_bytes=60 << 20
        ),
    )(queries, key_states, value_states, out_weight)


def solution(mesh):
    return jax.shard_map(
        local,
        mesh=mesh,
        in_specs=(P("seq", "head"), P("seq", "head"), P("seq", "head"), P("head", None)),
        out_specs=P("seq", "head"),
        check_vma=False,
    )
```

time: 92.2 us -> 71.2 us (0.77)
  Pallas kernels: 88.5 us -> 69.1 us
  local copies, waits for them, and re-layouts: 3.53 us -> 1.77 us
    pallas_call x1, Pallas kernels: 88.5 us -> 69.1 us  [local(): pl.pallas_call(kernel, out_shape=jax.ShapeDtypeStruct((T, 1024), bf16), i...]
    unnamed x7 -> x1, local copies, waits for them, and re-layouts: 3.53 us -> 1.77 us
where the time goes in v2:
time: 71.2 us; the launch traced here: 70.9 us
  Pallas kernels  69.1 us (97%)
  local copies, waits for them, and re-layouts  1.77 us (2%)
    pallas_call x1, Pallas kernels, local(): pl.pallas_call(kernel, out_shape=jax.ShapeDtypeStruct((T, 1024), bf16), i...  69.1 us
    unnamed x1, local copies, waits for them, and re-layouts  1.77 us

profile of v2, /device:TPU:1, one launch (start us, length us, event | category | flops | bytes accessed | tf_op | source)
XLA Modules:
  0.0 70.9 jit_solution(15248856460874768964)
XLA Ops:
  0.0 69.1 %shard_map.46 = bf16[192,1024]{1,0:T(8,128)(2,1)} custom-call(bf16[192,1024]{1,0:T(8,128)(2,1)} %q_ref.1, bf16[192,256]{1,0:T(8,128)(2,1)} %k_ref.1, bf16[192,256]{1,0:T(8,128)(2,1)} %v_ref.1, bf16[1024,4096]{1,0:T(8,128)(2,1)} %w_ref.1), custom_call_target="tpu_custom_call" | custom-call | tf_op jit(solution)/shard_map/pallas_call | solution.py:559
  69.1 1.8 %copy.6 = bf16[192,1024]{1,0:T(8,128)(2,1)} copy(bf16[192,1024]{1,0:T(8,128)(2,1)} %shard_map.46) | data formatting | bytes 786432

commit v3 on v2

--- a/solution.py
+++ b/solution.py
@@ -460,31 +460,45 @@
             value = jnp.dot(attin[rows, :], wv[j, :, cols], preferred_element_type=jnp.float32)
             ref[rows, cols] = value.astype(jnp.bfloat16)
 
-    first, second = pl.ds(0, H), pl.ds(H, H)
-    far_up = remote(po.at[0, first, :], ro.at[0], x_s.at[0], x_r.at[0], x_up)
-    far_down = remote(po.at[0, second, :], ro.at[1], x_s.at[1], x_r.at[1], x_down)
-    up_second = remote(pp.at[second, :], fp.at[second, :], x_s.at[2], x_r.at[2], x_up)
-    down_first = remote(pm.at[first, :], fm.at[first, :], x_s.at[3], x_r.at[3], x_down)
-    up_first = remote(pp.at[first, :], fp.at[first, :], x_s.at[4], x_r.at[4], x_up)
-    down_second = remote(pm.at[second, :], fm.at[second, :], x_s.at[5], x_r.at[5], x_down)
-    attended_ready(0)
-    project(0, 0, po.at[0])
-    far_up.start()
-    project(2, 0, pm)
-    down_first.start()
-    attended_ready(1)
-    project(0, 1, po.at[0])
-    far_down.start()
-    project(1, 1, pp)
-    up_second.start()
-    project(1, 0, pp)
-    far_up.wait_recv()
-    pp[0:H, :] = (pp[0:H, :].astype(jnp.float32) + ro[0].astype(jnp.float32)).astype(jnp.bfloat16)
-    up_first.start()
-    project(2, 1, pm)
-    far_down.wait_recv()
-    pm[H:T, :] = (pm[H:T, :].astype(jnp.float32) + ro[1].astype(jnp.float32)).astype(jnp.bfloat16)
-    down_second.start()
+    left, right = pl.ds(0, 512), pl.ds(512, 512)
+
+    def x_copies(part):
+        rows = pl.ds(part * H, H)
+
+        def copy(index, src, dst, to):
+            return remote(src, dst, x_s.at[index, part], x_r.at[index, part], to)
+
+        return (
+            copy(0, po.at[0, rows, left], ro.at[0, rows, :], x_up),
+            copy(1, po.at[0, rows, right], ro.at[1, rows, :], x_down),
+            copy(2, pp.at[rows, right], fp.at[rows, right], x_up),
+            copy(3, pm.at[rows, left], fm.at[rows, left], x_down),
+            copy(4, pp.at[rows, left], fp.at[rows, left], x_up),
+            copy(5, pm.at[rows, right], fm.at[rows, right], x_down),
+        )
+
+    shares = [x_copies(part) for part in range(2)]
+    for part in range(2):
+        far_up, far_down, up_plain, down_plain, up_sum, down_sum = shares[part]
+        attended_ready(part)
+        project(0, part, po.at[0])
+        far_up.start()
+        far_down.start()
+        project(1, part, pp)
+        up_plain.start()
+        project(2, part, pm)
+        down_plain.start()
+    for part in range(2):
+        far_up, far_down, up_plain, down_plain, up_sum, down_sum = shares[part]
+        rows = slice(part * H, (part + 1) * H)
+        far_up.wait_recv()
+        value = pp[rows, 0:512].astype(jnp.float32) + ro[0, rows, :].astype(jnp.float32)
+        pp[rows, 0:512] = value.astype(jnp.bfloat16)
+        up_sum.start()
+        far_down.wait_recv()
+        value = pm[rows, 512:1024].astype(jnp.float32) + ro[1, rows, :].astype(jnp.float32)
+        pm[rows, 512:1024] = value.astype(jnp.bfloat16)
+        down_sum.start()
     project(3, 0, po.at[1])
     project(3, 1, po.at[1])
 
@@ -493,14 +507,12 @@
         value = po[1, rows, :].astype(jnp.float32) + fp[rows, :].astype(jnp.float32)
         out_ref[rows, :] = (value + fm[rows, :].astype(jnp.float32)).astype(jnp.bfloat16)
 
-    down_first.wait_recv()
-    up_first.wait_recv()
-    total(0)
-    up_second.wait_recv()
-    down_second.wait_recv()
-    total(1)
-
-    for copy in (far_up, far_down, up_second, down_first, up_first, down_second, *pair_copies, *q_copies):
+    for part in range(2):
+        for copy in shares[part][2:]:
+            copy.wait_recv()
+        total(part)
+
+    for copy in (*shares[0], *shares[1], *pair_copies, *q_copies):
         copy.wait_send()
 
     for part in range(2):
@@ -573,13 +585,13 @@
             pltpu.VMEM((2, T, 1024), bf16),
             pltpu.VMEM((T, 1024), bf16),
             pltpu.VMEM((T, 1024), bf16),
-            pltpu.VMEM((2, T // 2, 1024), bf16),
+            pltpu.VMEM((2, T, 512), bf16),
             pltpu.VMEM((T, 1024), bf16),
             pltpu.VMEM((T, 1024), bf16),
             dma((4, 9)), dma((4, 9)), dma((4, 9)), dma((4, 9)),
             dma((10,)), dma((2,)), dma((2,)), dma((2,)),
             dma, dma((3,)), dma((3,)), dma((2,)), dma((2,)), dma((4,)),
-            dma((3, 2)), dma((3, 2)), dma((2,)), dma((6,)), dma((6,)),
+            dma((3, 2)), dma((3, 2)), dma((2,)), dma((6, 2)), dma((6, 2)),
         ],
         compiler_params=pltpu.CompilerParams(
             collective_id=0, has_side_effects=True, vmem_limit_bytes=60 << 20

time: 71.2 us -> 70.5 us (level)
  no operation moved by 1% of the time
where the time goes in v3:
time: 70.5 us; the launch traced here: 70.4 us
  Pallas kernels  68.6 us (97%)
  local copies, waits for them, and re-layouts  1.77 us (3%)
    pallas_call x1, Pallas kernels, local(): pl.pallas_call(kernel, out_shape=jax.ShapeDtypeStruct((T, 1024), bf16), i...  68.6 us
    unnamed x1, local copies, waits for them, and re-layouts  1.77 us

profile of v3, /device:TPU:1, one launch (start us, length us, event | category | flops | bytes accessed | tf_op | source)
XLA Modules:
  0.0 70.4 jit_solution(12047136596026432817)
XLA Ops:
  0.0 68.6 %shard_map.46 = bf16[192,1024]{1,0:T(8,128)(2,1)} custom-call(bf16[192,1024]{1,0:T(8,128)(2,1)} %q_ref.1, bf16[192,256]{1,0:T(8,128)(2,1)} %k_ref.1, bf16[192,256]{1,0:T(8,128)(2,1)} %v_ref.1, bf16[1024,4096]{1,0:T(8,128)(2,1)} %w_ref.1), custom_call_target="tpu_custom_call" | custom-call | tf_op jit(solution)/shard_map/pallas_call | solution.py:571
  68.6 1.8 %copy.6 = bf16[192,1024]{1,0:T(8,128)(2,1)} copy(bf16[192,1024]{1,0:T(8,128)(2,1)} %shard_map.46) | data formatting | bytes 786432

commit v4 on v3

--- a/solution.py
+++ b/solution.py
@@ -17,10 +17,10 @@
 
 
 def kernel(
-    q_ref, k_ref, v_ref, w_ref, out_ref,
-    kv, qraw, qs, acc, top, att, attin, wv, po, pp, pm, ro, fp, fm,
+    q_ref, k_ref, v_ref, w_ref, share_ref, fp, fm,
+    kv, qraw, qs, acc, top, att, attin, wv, po, pp, pm, ro,
     r_sem, s_sem, sr_sem, ss_sem, ys_sem, own_sem, part_r, part_s,
-    q_own, q_r, q_s, across_r, across_s, w_sem, att_r, att_s, att_own, x_r, x_s,
+    q_own, q_r, q_s, across_r, across_s, w_sem, att_r, att_s, att_own, x_r, x_s, share_sem,
 ):
     seq, x = lax.axis_index("seq"), lax.axis_index("head")
     y, z, c = seq // 16, (seq // 2) % Z, seq % 2
@@ -501,16 +501,12 @@
         down_sum.start()
     project(3, 0, po.at[1])
     project(3, 1, po.at[1])
-
-    def total(part):
-        rows = slice(part * H, (part + 1) * H)
-        value = po[1, rows, :].astype(jnp.float32) + fp[rows, :].astype(jnp.float32)
-        out_ref[rows, :] = (value + fm[rows, :].astype(jnp.float32)).astype(jnp.bfloat16)
-
+    own_share = pltpu.make_async_copy(po.at[1], share_ref, share_sem)
+    own_share.start()
     for part in range(2):
         for copy in shares[part][2:]:
             copy.wait_recv()
-        total(part)
+    own_share.wait()
 
     for copy in (*shares[0], *shares[1], *pair_copies, *q_copies):
         copy.wait_send()
@@ -568,11 +564,11 @@
     bf16, f32 = jnp.bfloat16, jnp.float32
     any_spec = pl.BlockSpec(memory_space=pl.ANY)
     dma = pltpu.SemaphoreType.DMA
-    return pl.pallas_call(
+    share, from_below, from_above = pl.pallas_call(
         kernel,
-        out_shape=jax.ShapeDtypeStruct((T, 1024), bf16),
+        out_shape=[jax.ShapeDtypeStruct((T, 1024), bf16)] * 3,
         in_specs=[any_spec] * 4,
-        out_specs=pl.BlockSpec(memory_space=pltpu.VMEM),
+        out_specs=[any_spec] * 3,
         scratch_shapes=[
             pltpu.VMEM((4, Z, 2, U, HEAD_DIM), bf16),
             pltpu.VMEM((2, U, 256), bf16),
@@ -586,17 +582,16 @@
             pltpu.VMEM((T, 1024), bf16),
             pltpu.VMEM((T, 1024), bf16),
             pltpu.VMEM((2, T, 512), bf16),
-            pltpu.VMEM((T, 1024), bf16),
-            pltpu.VMEM((T, 1024), bf16),
             dma((4, 9)), dma((4, 9)), dma((4, 9)), dma((4, 9)),
             dma((10,)), dma((2,)), dma((2,)), dma((2,)),
             dma, dma((3,)), dma((3,)), dma((2,)), dma((2,)), dma((4,)),
-            dma((3, 2)), dma((3, 2)), dma((2,)), dma((6, 2)), dma((6, 2)),
+            dma((3, 2)), dma((3, 2)), dma((2,)), dma((6, 2)), dma((6, 2)), dma,
         ],
         compiler_params=pltpu.CompilerParams(
             collective_id=0, has_side_effects=True, vmem_limit_bytes=60 << 20
         ),
     )(queries, key_states, value_states, out_weight)
+    return (share.astype(f32) + from_below.astype(f32) + from_above.astype(f32)).astype(bf16)
 
 
 def solution(mesh):

time: 70.5 us -> 70.2 us (level)
  other arithmetic: 0 us -> 2.18 us
  local copies, waits for them, and re-layouts: 1.77 us -> 0 us
    convert_element_type x0 -> x1, other arithmetic: none -> 2.18 us  [local(): (share.astype(f32) + from_below.astype(f32) + from_above.astype(f32)).ast...]
    unnamed x1 -> x0, local copies, waits for them, and re-layouts: 1.77 us -> none
where the time goes in v4:
time: 70.2 us; the launch traced here: 70.1 us
  Pallas kernels  67.9 us (97%)
  other arithmetic  2.18 us (3%)
    pallas_call x1, Pallas kernels, local(): pl.pallas_call(kernel, out_shape=[jax.ShapeDtypeStruct((T, 1024), bf16)]...  67.9 us
    convert_element_type x1, other arithmetic, local(): (share.astype(f32) + from_below.astype(f32) + from_above.astype(f32)).ast...  2.18 us

profile of v4, /device:TPU:1, one launch (start us, length us, event | category | flops | bytes accessed | tf_op | source)
XLA Modules:
  0.0 70.1 jit_solution(860349965193932622)
XLA Ops:
  0.0 67.9 %shard_map.46 = (bf16[192,1024]{1,0:T(8,128)(2,1)}, bf16[192,1024]{1,0:T(8,128)(2,1)}, bf16[192,1024]{1,0:T(8,128)(2,1)}) custom-call(bf16[192,1024]{1,0:T(8,128)(2,1)} %q_ref.1, bf16[192,256]{1,0:T(8,128)(2,1)} %k_ref.1, bf16[192,256]{1,0:T(8,128)(2,1)} %v_ref.1, bf16[1024,4096]{1,0:T(8,128)(2,1)} %w_ref.1), custom_call_target="tpu_custom_call" | custom-call | tf_op jit(solution)/shard_map/pallas_call | solution.py:567
  67.9 2.2 %add_convert_fusion = bf16[192,1024]{1,0:T(8,128)(2,1)} fusion(bf16[192,1024]{1,0:T(8,128)(2,1)} %get-tuple-element.10, bf16[192,1024]{1,0:T(8,128)(2,1)} %get-tuple-element.9, bf16[192,1024]{1,0:T(8,128)(2,1)} %get-tuple-element.8), kind=kLoop, calls=%fused_computation | loop fusion | flops 1179648 | bytes 1572864 | tf_op jit(solution)/shard_map/convert_element_type | solution.py:594

commit v5 on v4

--- a/solution.py
+++ b/solution.py
@@ -198,15 +198,15 @@
             qs[group, head * U : (head + 1) * U, 128:256] = low
 
     def queries_ready():
+        their = pl.ds(pl.multiple_of((1 - c) * T, T), T)
         my_q.wait()
-        their = pl.ds(pl.multiple_of((1 - c) * T, T), T)
-        for index, (group, rows, source) in enumerate(
-            ((late_home, their, sibling), (1 - late_home, mine, pair), (1 - late_home, their, pair_cross))
-        ):
-            ref = qraw.at[group, rows, :]
+        ref = qraw.at[late_home, their, :]
+        remote(ref, ref, q_s.at[0], q_r.at[0], sibling).wait_recv()
+        prepare(late_home)
+        for index, rows, source in ((1, mine, pair), (2, their, pair_cross)):
+            ref = qraw.at[1 - late_home, rows, :]
             remote(ref, ref, q_s.at[index], q_r.at[index], source).wait_recv()
-        prepare(0)
-        prepare(1)
+        prepare(1 - late_home)
 
     def update(group, tile, scores, values):
         rows = pl.ds(tile * TILE, TILE)

time: 70.2 us -> 70.2 us (level)
  no operation moved by 1% of the time
where the time goes in v5:
time: 70.2 us; the launch traced here: 70.1 us
  Pallas kernels  67.9 us (97%)
  other arithmetic  2.18 us (3%)
    pallas_call x1, Pallas kernels, local(): pl.pallas_call(kernel, out_shape=[jax.ShapeDtypeStruct((T, 1024), bf16)]...  67.9 us
    convert_element_type x1, other arithmetic, local(): (share.astype(f32) + from_below.astype(f32) + from_above.astype(f32)).ast...  2.18 us

profile of v5, /device:TPU:1, one launch (start us, length us, event | category | flops | bytes accessed | tf_op | source)
XLA Modules:
  0.0 70.1 jit_solution(9379653915012998788)
XLA Ops:
  0.0 67.9 %shard_map.46 = (bf16[192,1024]{1,0:T(8,128)(2,1)}, bf16[192,1024]{1,0:T(8,128)(2,1)}, bf16[192,1024]{1,0:T(8,128)(2,1)}) custom-call(bf16[192,1024]{1,0:T(8,128)(2,1)} %q_ref.1, bf16[192,256]{1,0:T(8,128)(2,1)} %k_ref.1, bf16[192,256]{1,0:T(8,128)(2,1)} %v_ref.1, bf16[1024,4096]{1,0:T(8,128)(2,1)} %w_ref.1), custom_call_target="tpu_custom_call" | custom-call | tf_op jit(solution)/shard_map/pallas_call | solution.py:567
  67.9 2.2 %add_convert_fusion = bf16[192,1024]{1,0:T(8,128)(2,1)} fusion(bf16[192,1024]{1,0:T(8,128)(2,1)} %get-tuple-element.10, bf16[192,1024]{1,0:T(8,128)(2,1)} %get-tuple-element.9, bf16[192,1024]{1,0:T(8,128)(2,1)} %get-tuple-element.8), kind=kLoop, calls=%fused_computation | loop fusion | flops 1179648 | bytes 1572864 | tf_op jit(solution)/shard_map/convert_element_type | solution.py:594
